TPU v7x, 512 devices: a whole 4x4x16 slice. The times are simulated.
512 devices in a mesh: rep: 8 (over y_lo, x), shard: 64 (over y_hi, z, core).
Axes of the slice: x: 4, y: 4 (y_hi: 2, y_lo: 2; y = y_hi * 2 + y_lo), z: 16, core: 2. Of those that a mesh axis runs over, the one named last changes fastest.
Arguments:
- hidden: bfloat16 [131072, 192], P(('rep', 'shard')), may hold values from -16 to 16
- cotangent: bfloat16 [131072, 5120], P(('rep', 'shard')), may hold values from -6 to 6
- master: float32 [192, 5120], P('shard'), may hold values from -0.078125 to 0.078125
- moment: float32 [192, 5120], P('shard'), may hold values from -6 to 6
- second: float32 [192, 5120], P('shard'), may hold values from 0.1 to 10
Outputs:
- input_grad: bfloat16 [131072, 192], P(('rep', 'shard'))
- master_new: float32 [192, 5120], P('shard')
- moment_new: float32 [192, 5120], P('shard')
- second_new: float32 [192, 5120], P('shard')
- updated_weights: bfloat16 [192, 5120], replicated
All inputs are finite; a program needn't handle non-finite values.
Results may differ from a plain program's by a relative error of at most 0.0059.
Values may be sent and summed in bfloat16 or wider, within the bound.
A program may use at most 64 MiB of HBM per device.

v0:
```python
import math

import jax
import jax.numpy as jnp
from jax import lax
from jax.sharding import PartitionSpec as P


def adam_update(master, moment, second, gradient):
    moment_new = 0.9 * moment + 0.1 * gradient
    second_new = 0.95 * second + 0.05 * gradient * gradient
    first_fix = moment_new / (1.0 - 0.9**10)
    second_fix = second_new / (1.0 - 0.95**10)
    master_new = master - 0.01 * (first_fix / (jnp.sqrt(second_fix) + 1e-08) + 0.1 * master)
    return (master_new, moment_new, second_new)


def local(hidden, cotangent, master, moment, second):
    rep_count = lax.axis_size("rep")
    shard_count = lax.axis_size("shard")
    factor = 1.0 / math.sqrt(hidden.shape[0] * rep_count * shard_count)
    weights = master.astype(jnp.bfloat16)
    input_grad = lax.dot_general(
        cotangent,
        lax.all_gather(weights, "shard", axis=0, tiled=True),
        (((1,), (1,)), ((), ())),
        preferred_element_type=jnp.float32,
    ).astype(jnp.bfloat16)
    partial_rows = lax.psum_scatter(
        lax.dot_general(
            hidden, cotangent, (((0,), (0,)), ((), ())), preferred_element_type=jnp.float32
        ),
        "shard",
        scatter_dimension=0,
        tiled=True,
    )
    grad_part = lax.psum(partial_rows.astype(jnp.bfloat16), "rep").astype(jnp.float32)
    gradient = grad_part * factor
    master_new, moment_new, second_new = adam_update(master, moment, second, gradient)
    updated_weights = lax.all_gather(master_new.astype(jnp.bfloat16), "shard", axis=0, tiled=True)
    return (input_grad, master_new, moment_new, second_new, updated_weights)


def solution(mesh):
    placed = (
        P(("rep", "shard"), None),
        P(("rep", "shard"), None),
        P("shard", None),
        P("shard", None),
        P("shard", None),
    )
    return jax.shard_map(
        local,
        mesh=mesh,
        in_specs=placed,
        out_specs=(
            P(("rep", "shard"), None),
            P("shard", None),
            P("shard", None),
            P("shard", None),
            P(),
        ),
        check_vma=False,
    )
```

profile of v0, /device:TPU:1, one launch (start us, length us, event | category | flops | bytes accessed | tf_op | source)
XLA Modules:
  0.0 648.9 jit_solution(7203513702345787603)
XLA Ops:
  7.2 0.0 copy-start
  7.2 0.0 all-gather.5.cloned.1.call-start
  7.2 1.7 copy-done
  8.9 3.4 fusion.5
  12.3 0.0 copy-start.1
  12.4 0.0 copy-start.2
  12.4 0.0 copy-start.3
  12.4 304.4 %all-reduce.2 = bf16[192,5120]{1,0:T(8,128)(2,1)} all-reduce(f32[192,5120]{1,0:T(8,128)} %fusion.5), channel_id=2, replica_groups=mesh['rep'=8,'shard'=64] {'shard'}, use_global_device_ids=true, to_apply=%region_0.0.clone | all-reduce | flops 983040 | bytes 5898240
  316.7 1.3 dynamic-slice
  318.7 1.0 dynamic-slice_convert_fusion
  319.6 26.5 %psum.7 = bf16[3,5120]{1,0:T(4,128)(2,1)S(1)} all-reduce(bf16[3,5120]{1,0:T(4,128)(2,1)S(1)} %dynamic-slice_convert_fusion), channel_id=1, replica_groups=mesh['rep'=8,'shard'=64] {'rep'}, use_global_device_ids=true, to_apply=%region_1.0 | all-reduce | flops 15360 | bytes 61440 | tf_op jit(solution)/shard_map/psum | solution.py:37
  346.1 0.0 copy-done.1
  346.2 0.0 copy-done.2
  346.2 0.0 copy-done.3
  346.2 0.8 convert_bitcast_fusion
  347.0 0.0 all-gather.5.cloned.1.call-update
  347.0 0.0 all-gather.7.cloned.1.call-start
  347.1 0.7 all-gather.7.cloned.1.call-update
  347.8 146.1 %all-gather.5.cloned.1.call-done = bf16[64,3,5120]{2,1,0:T(4,128)(2,1)} async-done(((bf16[1,3,5120]{2,1,0:T(4,128)(2,1)}), bf16[64,3,5120]{2,1,0:T(4,128)(2,1)}) %all-gather.5.cloned.1.call-update) | async-done | bytes 1966096 | tf_op jit(solution)/shard_map/all_gather | solution.py:25
  493.9 4.6 reshape.11
  498.5 3.2 convolution_convert_fusion
  501.7 135.8 %all-gather.7.cloned.1.call-done = bf16[64,3,5120]{2,1,0:T(4,128)(2,1)} async-done(((bf16[1,3,5120]{2,1,0:T(4,128)(2,1)}), bf16[64,3,5120]{2,1,0:T(4,128)(2,1)}) %all-gather.7.cloned.1.call-update) | async-done | bytes 1966096 | tf_op jit(solution)/shard_map/all_gather | solution.py:40
  637.5 4.6 reshape.13
Async XLA Ops:
  7.2 1.7 copy-start
  7.2 486.7 %all-gather.5.cloned.1.call-start = ((), (), s32[]{:S(2)}) async-start(), calls=%async_computation | async-start | bytes 2662400 | tf_op jit(solution)/shard_map/all_gather | solution.py:25
  12.3 333.8 %copy-start.1 = (f32[3,5120]{1,0:T(4,128)S(1)}, f32[3,5120]{1,0:T(4,128)}, u32[]{:S(2)}) copy-start(f32[3,5120]{1,0:T(4,128)} %param.7) | copy-start | bytes 184324
  12.4 333.8 %copy-start.2 = (f32[3,5120]{1,0:T(4,128)S(1)}, f32[3,5120]{1,0:T(4,128)}, u32[]{:S(2)}) copy-start(f32[3,5120]{1,0:T(4,128)} %param.8) | copy-start | bytes 184324
  12.4 333.8 %copy-start.3 = (f32[3,5120]{1,0:T(4,128)S(1)}, f32[3,5120]{1,0:T(4,128)}, u32[]{:S(2)}) copy-start(f32[3,5120]{1,0:T(4,128)} %param.9) | copy-start | bytes 184324
  347.0 290.5 %all-gather.7.cloned.1.call-start = ((), (), s32[]{:S(2)}) async-start(), calls=%async_computation.1 | async-start | bytes 2662400 | tf_op jit(solution)/shard_map/all_gather | solution.py:40
Sparse Core Ops, SparseCore 0:
  347.2 146.6 all-gather.4
  497.1 140.3 all-gather.6
where the time goes:
time: 649 us
  blocking collectives  331 us (51%)
  waiting for transfers between devices  283 us (44%)
  between operations  14.7 us (2%)
  local copies, waits for them, and re-layouts  13.1 us (2%)
  matrix products  6.65 us (1%)
    unnamed x1, blocking collectives  304 us
    all_gather x1, waiting for transfers between devices, local(): lax.all_gather(weights, 'shard', axis=0, tiled=True)  146 us
    all_gather x1, waiting for transfers between devices, local(): lax.all_gather(master_new.astype(jnp.bfloat16), 'shard', axis=0, tiled=True)  136 us
    psum x1, blocking collectives, local(): lax.psum(partial_rows.astype(jnp.bfloat16), 'rep').astype(jnp.float32)  26.5 us
  transfers between devices with their start and end apart: 2, of which 2 were waited for; matrix products, arithmetic and copies ran while one was open for 1% of the time, Pallas kernels for 0%

commit v1 on v0

v1 whole, which is shorter than its diff:
```python
import functools
import math

import jax
import jax.numpy as jnp
import numpy as np
from jax import lax
from jax.experimental import pallas as pl
from jax.experimental.pallas import tpu as pltpu
from jax.sharding import PartitionSpec as P

MESH = pl.DeviceIdType.MESH
BF16 = jnp.bfloat16
F32 = jnp.float32

NZ = 16
ROWS = 192
D = 5120
TOK = 256
OWN = 3
BR = OWN * NZ
BC = D // 8
NJ = BC // 128
TILE = 16

NEAR = (1, 3, 2)
FAR = (2, 1, 3)


def constants():
    order = np.zeros((ROWS, ROWS), np.float32)
    for c in range(2):
        for h in range(2):
            for z in range(NZ):
                for i in range(OWN):
                    order[c * 96 + h * BR + z * OWN + i, h * 96 + z * 6 + c * OWN + i] = 1.0
    tiles = np.zeros((NZ * TILE, NJ * BR), np.float32)
    for z in range(NZ):
        for j in range(NJ):
            for i in range(OWN):
                tiles[z * TILE + OWN * j + i, j * BR + z * OWN + i] = 1.0
    weave = np.zeros((2, 96, 96), np.float32)
    for core in range(2):
        for c in range(2):
            for z in range(NZ):
                for i in range(OWN):
                    weave[core, z * 6 + c * OWN + i, (0 if c == core else BR) + z * OWN + i] = 1.0
    return tuple(m.astype(BF16) for m in (order, tiles, tiles.T.copy(), weave))


def adam_update(master, moment, second, gradient):
    moment_new = 0.9 * moment + 0.1 * gradient
    second_new = 0.95 * second + 0.05 * gradient * gradient
    first_fix = moment_new / (1.0 - 0.9**10)
    second_fix = second_new / (1.0 - 0.95**10)
    master_new = master - 0.01 * (first_fix / (jnp.sqrt(second_fix) + 1e-08) + 0.1 * master)
    return (master_new, moment_new, second_new)


def dot(a, b):
    return jnp.dot(a, b, preferred_element_type=F32)


def dot_t(a, b):
    return lax.dot_general(a, b, (((1,), (1,)), ((), ())), preferred_element_type=F32)


def send(src, dst, sems, k, device):
    return pltpu.make_async_remote_copy(
        src_ref=src,
        dst_ref=dst,
        send_sem=sems.at[0, k],
        recv_sem=sems.at[1, k],
        device_id=device,
        device_id_type=MESH,
    )


def device(x, y, z, core):
    return (lax.rem(y, 2) * 4 + x, lax.div(y, 2) * 32 + z * 2 + core)


def kernel(
    factor,
    hidden, cot, master, moment, second, order, tiles, tiles_t, weave,
    ig_out, master_out, moment_out, second_out, weights_out,
    hidden_v, cot_v, master_v, moment_v, second_v, order_v, tiles_v, tiles_tv, weave_v,
    states, grads, pair_s, pair_r, mine, one_s, one_r, two_s, two_r,
    z_s, z_r, unit, w_z, u_z, w_own, w_sib, u_own, u_sib, w_full, u_full,
    grad_rows, master_n, moment_n, second_n, ig_sum, ig_v,
    in_sem, cot_sem, out_sem, full_sem,
    pair_sem, one_sem, two_sem, z_sem, rep_sem,
    wz_sem, w1_sem, w2_sem, wp_sem, uz_sem, u1_sem, u2_sem, up_sem,
):
    rep, shard = lax.axis_index("rep"), lax.axis_index("shard")
    x, y_lo = lax.rem(rep, 4), lax.div(rep, 4)
    core, z, y_hi = lax.rem(shard, 2), lax.rem(lax.div(shard, 2), NZ), lax.div(shard, 32)
    y = y_hi * 2 + y_lo
    first = core == 0

    def at_xy(dx, dy):
        return device(lax.rem(x + dx, 4), lax.rem(y + dy, 4), z, core)

    def along_one(d):
        return at_xy(jnp.where(first, d, 0), jnp.where(first, 0, d))

    def along_two(d):
        return at_xy(jnp.where(first, 0, d), jnp.where(first, d, 0))

    def along_z(d):
        return device(x, y, lax.rem(z + d, NZ), core)

    sibling = device(x, y, z, 1 - core)

    barrier = pltpu.get_barrier_semaphore()
    for d in (1, 2, 3):
        pl.semaphore_signal(barrier, inc=1, device_id=along_one(d), device_id_type=MESH)
        pl.semaphore_signal(barrier, inc=1, device_id=along_two(d), device_id_type=MESH)
    pl.semaphore_signal(barrier, inc=1, device_id=sibling, device_id_type=MESH)
    for d in range(1, NZ):
        pl.semaphore_signal(barrier, inc=1, device_id=along_z(d), device_id_type=MESH)

    loads = [
        pltpu.make_async_copy(src, dst, in_sem.at[k])
        for k, (src, dst) in enumerate(
            (
                (order, order_v),
                (hidden, hidden_v),
                (master, master_v),
                (moment, moment_v),
                (second, second_v),
                (tiles, tiles_v),
                (tiles_t, tiles_tv),
                (weave, weave_v),
            )
        )
    ]

    def cot_load(k):
        cols = pl.ds(k * BC, BC)
        return pltpu.make_async_copy(cot.at[:, cols], cot_v.at[:, cols], cot_sem.at[k])

    loads[0].start()
    loads[1].start()
    for k in range(8):
        cot_load(k).start()
    for load in loads[2:]:
        load.start()

    loads[0].wait()
    loads[1].wait()
    hidden_t = dot_t(order_v[...], hidden_v[...]).astype(BF16)
    for k in range(8):
        cot_load(k).wait()
        grads[k] = dot(hidden_t, cot_v[:, k * BC : (k + 1) * BC])

    for load in loads[2:]:
        load.wait()
    states[...] = jnp.zeros_like(states)
    for s, ref in enumerate((master_v, moment_v, second_v)):
        for j in range(NJ):
            cols = pl.ds(pl.multiple_of(rep * BC + j * 128, 128), 128)
            states[s, OWN * j : OWN * (j + 1), :] = ref[:, cols]
    w_z[z] = states[0].astype(BF16)

    def block(a, b, of_first):
        dx, dy = jnp.where(of_first, a, b), jnp.where(of_first, b, a)
        to_x, to_y = lax.rem(x + dx, 4), lax.rem(y + dy, 4)
        return lax.rem(to_y, 2) * 4 + to_x, lax.div(to_y, 2) * BR

    def pair_copy(k):
        return send(pair_s.at[k], pair_r.at[k], pair_sem, k, sibling)

    for b in FAR + (0,):
        for a in FAR + (0,):
            col, row = block(a, b, jnp.logical_not(first))
            rows = pl.ds(pl.multiple_of((1 - core) * 96 + row, 16), BR)
            pair_s[a * 4 + b] = grads[col, rows, :].astype(BF16)

    pl.semaphore_wait(barrier, 6 + 1 + NZ - 1)

    for b in FAR + (0,):
        for a in FAR + (0,):
            pair_copy(a * 4 + b).start()

    def spread_z(ref, sems, d):
        return send(ref.at[z], ref.at[z], sems, d - 1, along_z(d))

    for d in range(1, NZ):
        spread_z(w_z, wz_sem, d).start()

    def one_copy(a, b):
        k = (a - 1) * 4 + b
        return send(one_s.at[k], one_r.at[k], one_sem, k, along_one(a))

    def two_copy(b):
        return send(two_s.at[b - 1], two_r.at[b - 1], two_sem, b - 1, along_two(b))

    for b in FAR + (0,):
        for a in FAR + (0,):
            pair_copy(a * 4 + b).wait_recv()
            col, row = block(a, b, first)
            rows = pl.ds(pl.multiple_of(core * 96 + row, 16), BR)
            term = grads[col, rows, :] + pair_r[a * 4 + b].astype(F32)
            if a == 0:
                mine[b] = term
            else:
                one_s[(a - 1) * 4 + b] = term.astype(BF16)
                one_copy(a, b).start()

    for b in FAR + (0,):
        term = mine[b]
        for a in NEAR:
            one_copy(a, b).wait_recv()
            term += one_r[(a - 1) * 4 + b].astype(F32)
        if b == 0:
            mine[0] = term
        else:
            two_s[b - 1] = term.astype(BF16)
            two_copy(b).start()

    def gather_z(ref, own, sems):
        for d in range(1, NZ):
            spread_z(ref, sems, d).wait_recv()
        pieces = dot(tiles_tv[...], ref[...].reshape(NZ * TILE, 128)).astype(BF16)
        for j in range(NJ):
            own[0, :, j * 128 : (j + 1) * 128] = pieces[j * BR : (j + 1) * BR]

    def gather_two(own, sems, b):
        return send(own.at[0], own.at[b], sems, b - 1, along_two(b))

    def gather_one(own, sems, a, b):
        return send(own.at[b], own.at[a * 4 + b], sems, (a - 1) * 4 + b, along_one(a))

    def gather_pair(own, sib, sems, k):
        return send(own.at[k], sib.at[k], sems, k, sibling)

    def place(own, sib, full, dx, dy):
        from_x, from_y = lax.rem(x + 4 - dx, 4), lax.rem(y + 4 - dy, 4)
        k_own = jnp.where(first, dx * 4 + dy, dy * 4 + dx)
        k_sib = jnp.where(first, dy * 4 + dx, dx * 4 + dy)
        both = jnp.concatenate([own[k_own], sib[k_sib]], axis=0)
        rows = pl.ds(pl.multiple_of(lax.div(from_y, 2) * 96, 16), 96)
        cols = pl.ds(pl.multiple_of((lax.rem(from_y, 2) * 4 + from_x) * BC, 128), BC)
        full[rows, cols] = dot(weave_v[core], both).astype(BF16)
        return rows, cols

    gather_z(w_z, w_own, wz_sem)
    for b in FAR:
        gather_two(w_own, w1_sem, b).start()

    term = mine[0]
    for b in NEAR:
        two_copy(b).wait_recv()
        term += two_r[b - 1].astype(F32)
    total = term.astype(BF16)
    stacked = jnp.concatenate([total[:, j * 128 : (j + 1) * 128] for j in range(NJ)], axis=0)
    z_s[...] = dot(tiles_v[...], stacked).astype(BF16).reshape(NZ, TILE, 128)

    def z_copy(d):
        return send(z_s.at[lax.rem(z + d, NZ)], z_r.at[d - 1], z_sem, d - 1, along_z(d))

    for d in (8, 7, 9, 6, 10, 5, 11, 4, 12, 3, 13, 2, 14, 1, 15):
        z_copy(d).start()

    for b in (0,) + NEAR:
        if b:
            gather_two(w_own, w1_sem, b).wait_recv()
        for a in FAR:
            gather_one(w_own, w2_sem, a, b).start()
        gather_pair(w_own, w_sib, wp_sem, b).start()

    term = z_s[z].astype(F32)
    for d in range(1, NZ):
        z_copy(d).wait_recv()
        term += z_r[d - 1].astype(F32)
    gradient = term * factor
    unit[0] = gradient
    u_z[z] = adam_update(states[0], states[1], states[2], gradient)[0].astype(BF16)
    for d in (8, 7, 9, 6, 10, 5, 11, 4, 12, 3, 13, 2, 14, 1, 15):
        spread_z(u_z, uz_sem, d).start()

    def rep_x(d):
        return send(unit.at[0], unit.at[d], rep_sem, d - 1, at_xy(d, 0))

    other_y = device(x, y + 1 - 2 * y_lo, z, core)
    rep_y = send(unit.at[pl.ds(0, 4)], unit.at[pl.ds(4, 4)], rep_sem, 3, other_y)
    for d in FAR:
        rep_x(d).start()
    for d in NEAR:
        rep_x(d).wait_recv()
    rep_y.start()

    groups = (((1, 0), (3, 0), (2, 0)), ((1, 1), (3, 1), (2, 1)), ((1, 3), (3, 3), (2, 3)), ((1, 2), (3, 2), (2, 2)))
    ready = (
        ((0, 0), (0, 1), (1, 0), (0, 3), (3, 0), (0, 2), (2, 0)),
        ((1, 1),),
        ((1, 3), (3, 1), (3, 3)),
        ((1, 2), (2, 1), (3, 2), (2, 3), (2, 2)),
    )

    def gather_rest(own, sib, full, sems_two, sems_pair, done):
        for step in range(5):
            if step < 4:
                for a, b in groups[step]:
                    gather_one(own, sems_two, a, b).wait_recv()
                    gather_pair(own, sib, sems_pair, a * 4 + b).start()
            if step > 0:
                for dx, dy in ready[step - 1]:
                    k_sib = jnp.where(first, dy * 4 + dx, dx * 4 + dy)
                    gather_pair(own, sib, sems_pair, k_sib).wait_recv()
                    done(*place(own, sib, full, dx, dy), dx * 4 + dy)

    gather_rest(w_own, w_sib, w_full, w2_sem, wp_sem, lambda rows, cols, k: None)
    ig_sum[...] = dot_t(cot_v[:, 0:BC], w_full[:, 0:BC])

    def ig_step(k, carry):
        cols = pl.ds(pl.multiple_of(k * BC, 128), BC)
        ig_sum[...] += dot_t(cot_v[:, cols], w_full[:, cols])
        return carry

    lax.fori_loop(1, 8, ig_step, 0)
    ig_v[...] = ig_sum[...].astype(BF16)
    stores = [pltpu.make_async_copy(ig_v, ig_out, out_sem.at[0])]
    stores[0].start()

    rep_y.wait_recv()
    for e in range(2):
        for d in range(4):
            source = lax.rem(y_lo + e, 2) * 4 + lax.rem(x + 4 - d, 4)
            for j in range(NJ):
                cols = pl.ds(pl.multiple_of(source * BC + j * 128, 128), 128)
                grad_rows[:, cols] = unit[e * 4 + d, OWN * j : OWN * (j + 1), :]
    new = adam_update(master_v[...], moment_v[...], second_v[...], grad_rows[...])
    master_n[...], moment_n[...], second_n[...] = new
    for k, (src, dst) in enumerate(((master_n, master_out), (moment_n, moment_out), (second_n, second_out))):
        stores.append(pltpu.make_async_copy(src, dst, out_sem.at[k + 1]))
        stores[-1].start()

    gather_z(u_z, u_own, uz_sem)
    for b in FAR:
        gather_two(u_own, u1_sem, b).start()
    for b in (0,) + NEAR:
        if b:
            gather_two(u_own, u1_sem, b).wait_recv()
        for a in FAR:
            gather_one(u_own, u2_sem, a, b).start()
        gather_pair(u_own, u_sib, up_sem, b).start()

    def store_full(rows, cols, k):
        copy = pltpu.make_async_copy(u_full.at[rows, cols], weights_out.at[rows, cols], full_sem.at[k])
        copy.start()
        stores.append(copy)

    gather_rest(u_own, u_sib, u_full, u2_sem, up_sem, store_full)

    for store in stores:
        store.wait()
    for k in range(16):
        pair_copy(k).wait_send()
        gather_pair(w_own, w_sib, wp_sem, k).wait_send()
        gather_pair(u_own, u_sib, up_sem, k).wait_send()
    for a in (1, 2, 3):
        two_copy(a).wait_send()
        rep_x(a).wait_send()
        gather_two(w_own, w1_sem, a).wait_send()
        gather_two(u_own, u1_sem, a).wait_send()
        for b in range(4):
            one_copy(a, b).wait_send()
            gather_one(w_own, w2_sem, a, b).wait_send()
            gather_one(u_own, u2_sem, a, b).wait_send()
    rep_y.wait_send()
    for d in range(1, NZ):
        z_copy(d).wait_send()
        spread_z(w_z, wz_sem, d).wait_send()
        spread_z(u_z, uz_sem, d).wait_send()


def local(hidden, cotangent, master, moment, second):
    factor = 1.0 / math.sqrt(hidden.shape[0] * lax.axis_size("rep") * lax.axis_size("shard"))
    any_space = pl.BlockSpec(memory_space=pl.ANY)
    vmem = pltpu.VMEM
    dma = pltpu.SemaphoreType.DMA
    blocks = lambda n, dtype=BF16: vmem((n, BR, BC), dtype)
    z_tiles = lambda n, dtype=BF16: vmem((n, TILE, 128), dtype)
    owned = vmem((OWN, D), F32)
    consts = constants()
    return pl.pallas_call(
        functools.partial(kernel, factor),
        out_shape=(
            jax.ShapeDtypeStruct((TOK, ROWS), BF16),
            jax.ShapeDtypeStruct((OWN, D), F32),
            jax.ShapeDtypeStruct((OWN, D), F32),
            jax.ShapeDtypeStruct((OWN, D), F32),
            jax.ShapeDtypeStruct((ROWS, D), BF16),
        ),
        in_specs=[any_space] * 9,
        out_specs=(any_space,) * 5,
        scratch_shapes=[
            vmem((TOK, ROWS), BF16), vmem((TOK, D), BF16), owned, owned, owned,
            *(vmem(m.shape, BF16) for m in consts),
            z_tiles(3, F32), vmem((8, ROWS, BC), F32), blocks(16), blocks(16), blocks(4, F32),
            blocks(12), blocks(12), blocks(3), blocks(3),
            z_tiles(NZ), z_tiles(NZ - 1), z_tiles(8, F32), z_tiles(NZ), z_tiles(NZ),
            blocks(16), blocks(16), blocks(16), blocks(16),
            vmem((ROWS, D), BF16), vmem((ROWS, D), BF16),
            owned, owned, owned, owned, vmem((TOK, ROWS), F32), vmem((TOK, ROWS), BF16),
            dma((8,)), dma((8,)), dma((4,)), dma((16,)),
            dma((2, 16)), dma((2, 12)), dma((2, 3)), dma((2, NZ - 1)), dma((2, 4)),
            dma((2, NZ - 1)), dma((2, 3)), dma((2, 12)), dma((2, 16)),
            dma((2, NZ - 1)), dma((2, 3)), dma((2, 12)), dma((2, 16)),
        ],
        compiler_params=pltpu.CompilerParams(
            collective_id=0, has_side_effects=True, vmem_limit_bytes=40 * 2**20
        ),
        name="adamw_step",
    )(hidden, cotangent, master, moment, second, *(jnp.asarray(m) for m in consts))


def solution(mesh):
    placed = (
        P(("rep", "shard"), None),
        P(("rep", "shard"), None),
        P("shard", None),
        P("shard", None),
        P("shard", None),
    )
    return jax.shard_map(
        local,
        mesh=mesh,
        in_specs=placed,
        out_specs=(
            P(("rep", "shard"), None),
            P("shard", None),
            P("shard", None),
            P("shard", None),
            P(),
        ),
        check_vma=False,
    )
```

time: 649 us -> 78.3 us (0.12)
  blocking collectives: 331 us -> 0 us
  waiting for transfers between devices: 283 us -> 0 us
  Pallas kernels: 0 us -> 64.4 us
  between operations: 14.7 us -> 0.66 us
  matrix products: 6.65 us -> 0 us
    unnamed x1 -> x0, blocking collectives: 304 us -> none
    all_gather x2 -> x0, waiting for transfers between devices: 282 us -> none  [the longest x1 146 us: local(): lax.all_gather(weights, 'shard', axis=0, tiled=True)]
    pallas_call x0 -> x1, Pallas kernels: none -> 64.4 us  [local(): pl.pallas_call(functools.partial(kernel, factor), out_shape=(jax.ShapeDty...]
    psum x1 -> x0, blocking collectives: 26.5 us -> none  [local(): lax.psum(partial_rows.astype(jnp.bfloat16), 'rep').astype(jnp.float32)]
    dot_general x2 -> x0, matrix products: 6.65 us -> none  [the longest x1 3.44 us: local(): lax.dot_general(hidden, cotangent, (((0,), (0,)), ((), ())), preferred_el...]
  transfers between devices with their start and end apart: 2 -> 0, of which waited for: 2 -> 0; matrix products, arithmetic and copies ran while one was open for 1% -> 0% of each run, Pallas kernels for 0% -> 0%
where the time goes in v1:
time: 78.3 us; the launch traced here: 77.9 us
  Pallas kernels  64.4 us (82%)
  local copies, waits for them, and re-layouts  12.8 us (16%)
    pallas_call x1, Pallas kernels, local(): pl.pallas_call(functools.partial(kernel, factor), out_shape=(jax.ShapeDty...  64.4 us
    unnamed x21, local copies, waits for them, and re-layouts  12.1 us

profile of v1, /device:TPU:1, one launch (start us, length us, event | category | flops | bytes accessed | tf_op | source)
XLA Modules:
  0.0 77.9 jit_solution(807445472097487794)
XLA Ops:
  0.6 1.0 %copy.14.hidden = bf16[256,192]{1,0:T(8,128)(2,1)S(1)} copy(bf16[256,192]{0,1:T(8,128)(2,1)} %param.9) | data formatting | bytes 196608 | tf_op args[0]
  1.6 0.0 copy-start
  1.6 1.7 %copy-done = bf16[256,5120]{1,0:T(8,128)(2,1)S(1)} copy-done((bf16[256,5120]{1,0:T(8,128)(2,1)S(1)}, bf16[256,5120]{1,0:T(8,128)(2,1)}, u32[]{:S(2)}) %copy-start) | copy-done | bytes 2621464
  3.4 0.0 copy-start.1
  3.4 0.9 %copy-done.1 = bf16[256,240]{1,0:T(8,128)(2,1)S(1)} copy-done((bf16[256,240]{1,0:T(8,128)(2,1)S(1)}, bf16[256,240]{1,0:T(8,128)(2,1)}, u32[]{:S(2)}) %copy-start.1) | copy-done | bytes 122904
  4.3 0.0 copy-start.2
  4.3 0.9 %copy-done.2 = bf16[240,256]{1,0:T(8,128)(2,1)S(1)} copy-done((bf16[240,256]{1,0:T(8,128)(2,1)S(1)}, bf16[240,256]{1,0:T(8,128)(2,1)}, u32[]{:S(2)}) %copy-start.2) | copy-done | bytes 122904
  5.2 0.0 copy-start.3
  5.2 0.9 %copy-done.3 = bf16[192,192]{1,0:T(8,128)(2,1)S(1)} copy-done((bf16[192,192]{1,0:T(8,128)(2,1)S(1)}, bf16[192,192]{1,0:T(8,128)(2,1)}, u32[]{:S(2)}) %copy-start.3) | copy-done | bytes 73752
  6.1 0.0 copy-start.4
  6.1 0.9 %copy-done.4 = f32[3,5120]{1,0:T(4,128)S(1)} copy-done((f32[3,5120]{1,0:T(4,128)S(1)}, f32[3,5120]{1,0:T(4,128)}, u32[]{:S(2)}) %copy-start.4) | copy-done | bytes 61464
  7.0 0.0 copy-start.5
  7.0 0.9 %copy-done.5 = f32[3,5120]{1,0:T(4,128)S(1)} copy-done((f32[3,5120]{1,0:T(4,128)S(1)}, f32[3,5120]{1,0:T(4,128)}, u32[]{:S(2)}) %copy-start.5) | copy-done | bytes 61464
  7.8 0.0 copy-start.6
  7.8 0.9 %copy-done.6 = f32[3,5120]{1,0:T(4,128)S(1)} copy-done((f32[3,5120]{1,0:T(4,128)S(1)}, f32[3,5120]{1,0:T(4,128)}, u32[]{:S(2)}) %copy-start.6) | copy-done | bytes 61464
  8.7 0.0 copy-start.7
  8.7 0.8 %copy-done.7 = bf16[2,96,96]{2,1,0:T(8,128)(2,1)S(1)} copy-done((bf16[2,96,96]{2,1,0:T(8,128)(2,1)S(1)}, bf16[2,96,96]{2,1,0:T(8,128)(2,1)}, u32[]{:S(2)}) %copy-start.7) | copy-done | bytes 36888
  9.5 64.4 %adamw_step.1 = (bf16[256,192]{1,0:T(8,128)(2,1)S(1)}, f32[3,5120]{1,0:T(4,128)S(1)}, f32[3,5120]{1,0:T(4,128)S(1)}, f32[3,5120]{1,0:T(4,128)S(1)}, bf16[192,5120]{1,0:T(8,128)(2,1)S(1)}) custom-call(bf16[256,192]{1,0:T(8,128)(2,1)S(1)} %copy.14.hidden, bf16[256,5120]{1,0:T(8,128)(2,1)S(1)} %copy-done, f32[3,5120]{1,0:T(4,128)S(1)} %copy-done.4, ...), custom_call_target="tpu_custom_call" | custom-call | tf_op jit(solution)/shard_map/adamw_step/pallas_call | solution.py:388
  74.0 0.7 copy.15
  74.7 0.6 copy.20
  75.3 0.6 copy.21
  76.0 0.6 copy.22
  76.6 1.3 %copy.23 = bf16[192,5120]{1,0:T(8,128)(2,1)} copy(bf16[192,5120]{1,0:T(8,128)(2,1)S(1)} %get-tuple-element.19) | data formatting | bytes 3932160
Async XLA Ops:
  1.6 1.7 %copy-start = (bf16[256,5120]{1,0:T(8,128)(2,1)S(1)}, bf16[256,5120]{1,0:T(8,128)(2,1)}, u32[]{:S(2)}) copy-start(bf16[256,5120]{1,0:T(8,128)(2,1)} %cot.1) | copy-start | bytes 7864324
  3.4 0.9 %copy-start.1 = (bf16[256,240]{1,0:T(8,128)(2,1)S(1)}, bf16[256,240]{1,0:T(8,128)(2,1)}, u32[]{:S(2)}) copy-start(bf16[256,240]{1,0:T(8,128)(2,1)} %constant.9.clone.tiles) | copy-start | bytes 368644
  4.3 0.9 %copy-start.2 = (bf16[240,256]{1,0:T(8,128)(2,1)S(1)}, bf16[240,256]{1,0:T(8,128)(2,1)}, u32[]{:S(2)}) copy-start(bf16[240,256]{1,0:T(8,128)(2,1)} %constant.10.clone.tiles_t) | copy-start | bytes 368644
  5.2 0.9 %copy-start.3 = (bf16[192,192]{1,0:T(8,128)(2,1)S(1)}, bf16[192,192]{1,0:T(8,128)(2,1)}, u32[]{:S(2)}) copy-start(bf16[192,192]{1,0:T(8,128)(2,1)} %constant.8.clone.order) | copy-start | bytes 221188
  6.1 0.9 %copy-start.4 = (f32[3,5120]{1,0:T(4,128)S(1)}, f32[3,5120]{1,0:T(4,128)}, u32[]{:S(2)}) copy-start(f32[3,5120]{1,0:T(4,128)} %master.1) | copy-start | bytes 184324
  7.0 0.9 %copy-start.5 = (f32[3,5120]{1,0:T(4,128)S(1)}, f32[3,5120]{1,0:T(4,128)}, u32[]{:S(2)}) copy-start(f32[3,5120]{1,0:T(4,128)} %moment.1) | copy-start | bytes 184324
  7.8 0.9 %copy-start.6 = (f32[3,5120]{1,0:T(4,128)S(1)}, f32[3,5120]{1,0:T(4,128)}, u32[]{:S(2)}) copy-start(f32[3,5120]{1,0:T(4,128)} %second.1) | copy-start | bytes 184324
  8.7 0.8 %copy-start.7 = (bf16[2,96,96]{2,1,0:T(8,128)(2,1)S(1)}, bf16[2,96,96]{2,1,0:T(8,128)(2,1)}, u32[]{:S(2)}) copy-start(bf16[2,96,96]{2,1,0:T(8,128)(2,1)} %constant.11.clone.weave) | copy-start | bytes 110596

commit v2 on v0

v2 whole, which is shorter than its diff:
```python
import functools
import math

import jax
import jax.numpy as jnp
import numpy as np
from jax import lax
from jax.experimental import pallas as pl
from jax.experimental.pallas import tpu as pltpu
from jax.sharding import PartitionSpec as P

MESH = pl.DeviceIdType.MESH
BF16 = jnp.bfloat16
F32 = jnp.float32

NZ = 16
ROWS = 192
D = 5120
TOK = 256
OWN = 3
BR = OWN * NZ
BC = D // 8
NJ = BC // 128
TILE = 16

NEAR = (1, 3, 2)
FAR = (2, 1, 3)
Z_ORDER = (8, 7, 9, 6, 10, 5, 11, 4, 12, 3, 13, 2, 14, 1, 15)
LAG = 4


def constants():
    order = np.zeros((ROWS, ROWS), np.float32)
    for c in range(2):
        for h in range(2):
            for z in range(NZ):
                for i in range(OWN):
                    order[c * 96 + h * BR + z * OWN + i, h * 96 + z * 6 + c * OWN + i] = 1.0
    tiles = np.zeros((NZ * TILE, NJ * BR), np.float32)
    for z in range(NZ):
        for j in range(NJ):
            for i in range(OWN):
                tiles[z * TILE + OWN * j + i, j * BR + z * OWN + i] = 1.0
    weave = np.zeros((2, 96, 96), np.float32)
    for core in range(2):
        for c in range(2):
            for z in range(NZ):
                for i in range(OWN):
                    weave[core, z * 6 + c * OWN + i, (0 if c == core else BR) + z * OWN + i] = 1.0
    return tuple(m.astype(BF16) for m in (order, tiles, tiles.T.copy(), weave))


def adam_update(master, moment, second, gradient):
    moment_new = 0.9 * moment + 0.1 * gradient
    second_new = 0.95 * second + 0.05 * gradient * gradient
    first_fix = moment_new / (1.0 - 0.9**10)
    second_fix = second_new / (1.0 - 0.95**10)
    master_new = master - 0.01 * (first_fix / (jnp.sqrt(second_fix) + 1e-08) + 0.1 * master)
    return (master_new, moment_new, second_new)


def dot(a, b):
    return jnp.dot(a, b, preferred_element_type=F32)


def dot_t(a, b):
    return lax.dot_general(a, b, (((1,), (1,)), ((), ())), preferred_element_type=F32)


def device(x, y, z, core):
    return (lax.rem(y, 2) * 4 + x, lax.div(y, 2) * 32 + z * 2 + core)


def kernel(
    factor,
    hidden, cot, master, moment, second, order, tiles, tiles_t, weave,
    ig_out, master_out, moment_out, second_out, weights_out,
    hidden_v, cot_v, master_v, moment_v, second_v, order_v, tiles_v, tiles_tv, weave_v,
    states, grads, pair_s, pair_r, mine, one_s, one_r, two_s, two_r,
    z_s, z_r, unit, w_z, u_z, w_own, w_sib, u_own, u_sib, w_full, grad_rows, ig_sum,
    in_sem, cot_sem, sent, pair_sem, one_sem, two_sem, z_sem, rep_sem, w_sem, u_sem, hello,
):
    rep, shard = lax.axis_index("rep"), lax.axis_index("shard")
    x, y_lo = lax.rem(rep, 4), lax.div(rep, 4)
    core, z, y_hi = lax.rem(shard, 2), lax.rem(lax.div(shard, 2), NZ), lax.div(shard, 32)
    y = y_hi * 2 + y_lo
    first = core == 0

    def at_xy(dx, dy):
        return device(lax.rem(x + dx, 4), lax.rem(y + dy, 4), z, core)

    def along_one(d):
        return at_xy(jnp.where(first, d, 0), jnp.where(first, 0, d))

    def along_two(d):
        return at_xy(jnp.where(first, 0, d), jnp.where(first, d, 0))

    def along_z(d):
        return device(x, y, lax.rem(z + d, NZ), core)

    sibling = device(x, y, z, 1 - core)

    def send(src, dst, family, recv, to):
        return pltpu.make_async_remote_copy(
            src_ref=src, dst_ref=dst, send_sem=sent.at[family], recv_sem=recv, device_id=to, device_id_type=MESH
        )

    def received(ref, recv):
        send(ref, ref, 0, recv, sibling).wait_recv()

    def signal(sem, to):
        pl.semaphore_signal(sem, inc=1, device_id=to, device_id_type=MESH)

    barrier = pltpu.get_barrier_semaphore()
    signal(barrier, sibling)
    for d in (2, 1, 3):
        signal(barrier, along_one(d))
        signal(barrier, along_two(d))
    for d in (2, NZ - 2, 1, NZ - 1):
        signal(barrier, along_z(d))

    loads = [
        pltpu.make_async_copy(src, dst, in_sem.at[k])
        for k, (src, dst) in enumerate(
            (
                (order, order_v),
                (hidden, hidden_v),
                (master, master_v),
                (moment, moment_v),
                (second, second_v),
                (tiles, tiles_v),
                (tiles_t, tiles_tv),
                (weave, weave_v),
            )
        )
    ]
    steps = [(dx, e) for dx in FAR + (0,) for e in (1, 0)]

    def cot_cols(dx, e):
        col = lax.rem(y_lo + e, 2) * 4 + lax.rem(x + dx, 4)
        return pl.ds(pl.multiple_of(col * BC, 128), BC)

    def cot_load(t):
        cols = cot_cols(*steps[t])
        return pltpu.make_async_copy(cot.at[:, cols], cot_v.at[:, cols], cot_sem.at[t])

    loads[0].start()
    loads[1].start()
    for t in range(8):
        cot_load(t).start()
    for load in loads[2:]:
        load.start()

    def local_term(t):
        cot_load(t).wait()
        grads[t] = dot(hidden_t, cot_v[:, cot_cols(*steps[t])])
        pair_s[t] = grads[t, pl.ds(pl.multiple_of((1 - core) * 96, 16), 96), :].astype(BF16)

    def pair_copy(t):
        return send(pair_s.at[t], pair_r.at[t], 0, pair_sem.at[t], sibling)

    def first_axis(t):
        pair_copy(t).wait_recv()
        dx, e = steps[t]
        for dy in (e, e + 2):
            row = lax.div(lax.rem(y + dy, 4), 2) * BR
            a, b = jnp.where(first, dx, dy), jnp.where(first, dy, dx)

            def term():
                own = grads[t, pl.ds(pl.multiple_of(core * 96 + row, 16), BR), :]
                return own + pair_r[t, pl.ds(pl.multiple_of(row, 16), BR), :].astype(F32)

            def keep():
                mine[b] = term()

            def pass_on():
                k = b * 3 + a - 1
                one_s[k] = term().astype(BF16)
                send(one_s.at[k], one_r.at[k], 1, one_sem.at[b], along_one(a)).start()

            if dx and dy:
                pass_on()
            elif dx == dy:
                keep()
            else:
                pl.when(a == 0)(keep)
                pl.when(a != 0)(pass_on)

    loads[0].wait()
    loads[1].wait()
    hidden_t = dot(order_v[...], hidden_v[...]).astype(BF16)
    for t in range(8):
        local_term(t)
        if t == 0:
            pl.semaphore_wait(barrier, 1 + 6 + 4)
            signal(hello.at[0], along_z(2))
            signal(hello.at[0], along_z(NZ - 2))
        pair_copy(t).start()
        if t >= LAG:
            first_axis(t - LAG)

    for load in loads[2:]:
        load.wait()
    states[...] = jnp.zeros_like(states)
    for s, ref in enumerate((master_v, moment_v, second_v)):
        for j in range(NJ):
            cols = pl.ds(pl.multiple_of(rep * BC + j * 128, 128), 128)
            states[s, OWN * j : OWN * (j + 1), :] = ref[:, cols]
    w_z[z] = states[0].astype(BF16)

    pl.semaphore_wait(hello.at[0], 2)
    signal(hello.at[1], along_z(4))
    signal(hello.at[1], along_z(NZ - 4))
    for t in range(8 - LAG, 8):
        first_axis(t)
    pl.semaphore_wait(hello.at[1], 2)

    def spread_z(ref, family, recv):
        for d in Z_ORDER:
            send(ref.at[z], ref.at[z], family, recv, along_z(d)).start()

    spread_z(w_z, 4, w_sem.at[0])

    for b in FAR + (0,):
        received(one_r.at[3 * b : 3 * b + 3], one_sem.at[b])
        term = mine[b]
        for k in range(3 * b, 3 * b + 3):
            term += one_r[k].astype(F32)
        if b == 0:
            mine[0] = term
        else:
            two_s[b - 1] = term.astype(BF16)
            send(two_s.at[b - 1], two_r.at[b - 1], 2, two_sem.at[0], along_two(b)).start()
    received(two_r, two_sem.at[0])
    term = mine[0]
    for b in NEAR:
        term += two_r[b - 1].astype(F32)

    total = term.astype(BF16)
    stacked = jnp.concatenate([total[:, j * 128 : (j + 1) * 128] for j in range(NJ)], axis=0)
    z_s[...] = dot(tiles_v[...], stacked).astype(BF16).reshape(NZ, TILE, 128)
    for d in Z_ORDER:
        send(z_s.at[lax.rem(z + d, NZ)], z_r.at[d - 1], 3, z_sem.at[0], along_z(d)).start()

    def gather_z(ref, own, sem):
        received(ref.at[0 : NZ - 1], sem.at[0])
        pieces = dot(tiles_tv[...], ref[...].reshape(NZ * TILE, 128)).astype(BF16)
        for j in range(NJ):
            own[0, :, j * 128 : (j + 1) * 128] = pieces[j * BR : (j + 1) * BR]

    def gather_two(own, family, sem):
        for b in FAR:
            send(own.at[0], own.at[4 * b], family + 1, sem.at[b], along_two(b)).start()

    def gather_one(own, family, sem, b):
        if b:
            received(own.at[4 * b], sem.at[b])
        for a in FAR:
            send(own.at[4 * b], own.at[4 * b + a], family + 2, sem.at[4 + b], along_one(a)).start()

    def gather_pair(own, sib, family, sem, b):
        received(own.at[4 * b + 1 : 4 * b + 4], sem.at[4 + b])
        four = pl.ds(4 * b, 4)
        send(own.at[four], sib.at[four], family + 3, sem.at[8 + b], sibling).start()

    def pair_there(sib, sem, b):
        received(sib.at[4 * b : 4 * b + 4], sem.at[8 + b])

    def place(own, sib, full, dx, dy):
        from_x, from_y = lax.rem(x + 4 - dx, 4), lax.rem(y + 4 - dy, 4)
        k_own = jnp.where(first, dy * 4 + dx, dx * 4 + dy)
        k_sib = jnp.where(first, dx * 4 + dy, dy * 4 + dx)
        both = jnp.concatenate([own[k_own], sib[k_sib]], axis=0)
        rows = pl.ds(pl.multiple_of(lax.div(from_y, 2) * 96, 16), 96)
        cols = pl.ds(pl.multiple_of((lax.rem(from_y, 2) * 4 + from_x) * BC, 128), BC)
        full[rows, cols] = dot(weave_v[core], both).astype(BF16)

    gather_z(w_z, w_own, w_sem)
    gather_two(w_own, 4, w_sem)
    for b in (0,) + NEAR:
        gather_one(w_own, 4, w_sem, b)

    received(z_r, z_sem.at[0])
    term = z_s[z].astype(F32)
    for k in range(NZ - 1):
        term += z_r[k].astype(F32)
    gradient = term * factor
    unit[0] = gradient
    u_z[z] = adam_update(states[0], states[1], states[2], gradient)[0].astype(BF16)
    spread_z(u_z, 8, u_sem.at[0])

    for d in FAR:
        send(unit.at[0], unit.at[d], 12, rep_sem.at[0], at_xy(d, 0)).start()
    received(unit.at[1:4], rep_sem.at[0])
    other_y = device(x, y + 1 - 2 * y_lo, z, core)
    rep_y = send(unit.at[pl.ds(0, 4)], unit.at[pl.ds(4, 4)], 13, rep_sem.at[1], other_y)
    rep_y.start()

    for b in (0,) + NEAR:
        gather_pair(w_own, w_sib, 4, w_sem, b)

    rep_y.wait_recv()
    for e in range(2):
        for d in range(4):
            source = lax.rem(y_lo + e, 2) * 4 + lax.rem(x + 4 - d, 4)
            for j in range(NJ):
                cols = pl.ds(pl.multiple_of(source * BC + j * 128, 128), 128)
                grad_rows[:, cols] = unit[e * 4 + d, OWN * j : OWN * (j + 1), :]
    new = adam_update(master_v[...], moment_v[...], second_v[...], grad_rows[...])
    master_out[...], moment_out[...], second_out[...] = new

    gather_z(u_z, u_own, u_sem)
    gather_two(u_own, 8, u_sem)
    gather_one(u_own, 8, u_sem, 0)
    for b in range(4):
        pair_there(w_sib, w_sem, b)
    for dx in range(4):
        for dy in range(4):
            place(w_own, w_sib, w_full, dx, dy)
    for b in NEAR:
        gather_one(u_own, 8, u_sem, b)

    ig_sum[...] = dot_t(w_full[:, 0:BC], cot_v[:, 0:BC])

    def ig_step(k, carry):
        cols = pl.ds(pl.multiple_of(k * BC, 128), BC)
        ig_sum[...] += dot_t(w_full[:, cols], cot_v[:, cols])
        return carry

    lax.fori_loop(1, 8, ig_step, 0)
    ig_out[...] = ig_sum[...].astype(BF16)

    ready = (
        ((0, 0),),
        ((0, 1), (1, 0), (1, 1)),
        ((0, 3), (3, 0), (1, 3), (3, 1), (3, 3)),
        ((0, 2), (2, 0), (1, 2), (2, 1), (3, 2), (2, 3), (2, 2)),
    )
    bs = (0,) + NEAR
    for k in range(5):
        if k < 4:
            gather_pair(u_own, u_sib, 8, u_sem, bs[k])
        if k > 0:
            pair_there(u_sib, u_sem, bs[k - 1])
            for dx, dy in ready[k - 1]:
                place(u_own, u_sib, weights_out, dx, dy)

    tiles_of = lambda ref: ref.at[0 : NZ - 1]
    for family, ref in (
        (0, pair_s), (1, one_s), (2, two_s), (3, z_r),
        (4, tiles_of(w_z)), (5, w_own.at[0:3]), (6, w_own.at[0:12]), (7, w_own),
        (8, tiles_of(u_z)), (9, u_own.at[0:3]), (10, u_own.at[0:12]), (11, u_own),
        (12, unit.at[1:4]), (13, unit.at[0:4]),
    ):
        send(ref, ref, family, pair_sem.at[0], sibling).wait_send()


def write_out(*refs):
    n = len(refs) // 2
    sems = refs[-1]
    copies = [pltpu.make_async_copy(refs[k], refs[n + k], sems.at[k]) for k in range(n)]
    for copy in copies:
        copy.start()
    for copy in copies:
        copy.wait()


def local(hidden, cotangent, master, moment, second):
    factor = 1.0 / math.sqrt(hidden.shape[0] * lax.axis_size("rep") * lax.axis_size("shard"))
    any_space = pl.BlockSpec(memory_space=pl.ANY)
    vmem = pltpu.VMEM
    dma = pltpu.SemaphoreType.DMA
    blocks = lambda n, dtype=BF16: vmem((n, BR, BC), dtype)
    z_tiles = lambda n, dtype=BF16: vmem((n, TILE, 128), dtype)
    owned = vmem((OWN, D), F32)
    pairs = vmem((8, 2 * BR, BC), BF16)
    in_hbm = lambda a: pltpu.with_memory_space_constraint(a, pltpu.HBM)
    consts = constants()
    results = pl.pallas_call(
        functools.partial(kernel, factor),
        out_shape=(vmem((ROWS, TOK), BF16), owned, owned, owned, vmem((ROWS, D), BF16)),
        in_specs=[pl.BlockSpec(memory_space=pltpu.HBM)] * 9,
        out_specs=(pl.BlockSpec(memory_space=vmem),) * 5,
        scratch_shapes=[
            vmem((ROWS, TOK), BF16), vmem((TOK, D), BF16), owned, owned, owned,
            *(vmem(m.shape, BF16) for m in consts),
            z_tiles(3, F32), vmem((8, ROWS, BC), F32), pairs, pairs, blocks(4, F32),
            blocks(12), blocks(12), blocks(3), blocks(3),
            z_tiles(NZ), z_tiles(NZ - 1), z_tiles(8, F32), z_tiles(NZ), z_tiles(NZ),
            blocks(16), blocks(16), blocks(16), blocks(16),
            vmem((ROWS, D), BF16), owned, vmem((ROWS, TOK), F32),
            dma((8,)), dma((8,)), dma((14,)), dma((8,)), dma((4,)), dma((1,)), dma((1,)), dma((2,)),
            dma((12,)), dma((12,)), pltpu.SemaphoreType.REGULAR((2,)),
        ],
        compiler_params=pltpu.CompilerParams(
            collective_id=0, has_side_effects=True, vmem_limit_bytes=40 * 2**20
        ),
        name="adamw_step",
    )(*(in_hbm(a) for a in (hidden.T, cotangent, master, moment, second, *map(jnp.asarray, consts))))
    input_grad_t, *rest = pl.pallas_call(
        write_out,
        out_shape=tuple(pltpu.HBM(r.shape, r.dtype) for r in results),
        in_specs=[pl.BlockSpec(memory_space=pltpu.VMEM)] * 5,
        out_specs=(pl.BlockSpec(memory_space=pltpu.HBM),) * 5,
        scratch_shapes=[dma((5,))],
        name="write_out",
    )(*(pltpu.with_memory_space_constraint(r, pltpu.VMEM) for r in results))
    return (input_grad_t.T, *rest)


def solution(mesh):
    placed = (
        P(("rep", "shard"), None),
        P(("rep", "shard"), None),
        P("shard", None),
        P("shard", None),
        P("shard", None),
    )
    return jax.shard_map(
        local,
        mesh=mesh,
        in_specs=placed,
        out_specs=(
            P(("rep", "shard"), None),
            P("shard", None),
            P("shard", None),
            P("shard", None),
            P(),
        ),
        check_vma=False,
    )
```

time: 649 us -> 66.1 us (0.10)
  blocking collectives: 331 us -> 0 us
  waiting for transfers between devices: 283 us -> 0 us
  Pallas kernels: 0 us -> 65.3 us
  between operations: 14.7 us -> 0.64 us
  local copies, waits for them, and re-layouts: 13.1 us -> 0 us
  matrix products: 6.65 us -> 0 us
    unnamed x1 -> x0, blocking collectives: 304 us -> none
    all_gather x2 -> x0, waiting for transfers between devices: 282 us -> none  [the longest x1 146 us: local(): lax.all_gather(weights, 'shard', axis=0, tiled=True)]
    pallas_call x0 -> x2, Pallas kernels: none -> 65.3 us  [the longest x1 63.9 us: local(): pl.pallas_call(functools.partial(kernel, factor), out_shape=(vmem((ROWS,...]
    psum x1 -> x0, blocking collectives: 26.5 us -> none  [local(): lax.psum(partial_rows.astype(jnp.bfloat16), 'rep').astype(jnp.float32)]
    unnamed x11 -> x0, local copies, waits for them, and re-layouts: 12.2 us -> none
    dot_general x2 -> x0, matrix products: 6.65 us -> none  [the longest x1 3.44 us: local(): lax.dot_general(hidden, cotangent, (((0,), (0,)), ((), ())), preferred_el...]
  transfers between devices with their start and end apart: 2 -> 0, of which waited for: 2 -> 0; matrix products, arithmetic and copies ran while one was open for 1% -> 0% of each run, Pallas kernels for 0% -> 0%
where the time goes in v2:
time: 66.1 us; the launch traced here: 66 us
  Pallas kernels  65.3 us (99%)
    pallas_call x1, Pallas kernels, local(): pl.pallas_call(functools.partial(kernel, factor), out_shape=(vmem((ROWS,...  63.9 us
    pallas_call x1, Pallas kernels, local(): pl.pallas_call(write_out, out_shape=tuple((pltpu.HBM(r.shape, r.dtype) fo...  1.43 us

profile of v2, /device:TPU:1, one launch (start us, length us, event | category | flops | bytes accessed | tf_op | source)
XLA Modules:
  0.0 66.0 jit_solution(15865069582399753606)
XLA Ops:
  0.6 63.9 %adamw_step.1 = (bf16[192,256]{1,0:T(8,128)(2,1)S(1)}, f32[3,5120]{1,0:T(4,128)S(1)}, f32[3,5120]{1,0:T(4,128)S(1)}, f32[3,5120]{1,0:T(4,128)S(1)}, bf16[192,5120]{1,0:T(8,128)(2,1)S(1)}) custom-call(bf16[192,256]{1,0:T(8,128)(2,1)} %bitcast.2, bf16[256,5120]{1,0:T(8,128)(2,1)} %cot.1, f32[3,5120]{1,0:T(4,128)} %master.1, f32[3,5120]{1,0:T(4,128)} %moment.1, ...), custom_call_target="tpu_custom_call" | custom-call | tf_op jit(solution)/shard_map/adamw_step/pallas_call | solution.py:379
  64.6 1.4 %write_out.1 = (bf16[192,256]{1,0:T(8,128)(2,1)}, f32[3,5120]{1,0:T(4,128)}, f32[3,5120]{1,0:T(4,128)}, f32[3,5120]{1,0:T(4,128)}, bf16[192,5120]{1,0:T(8,128)(2,1)}) custom-call(bf16[192,256]{1,0:T(8,128)(2,1)S(1)} %get-tuple-element.15.refs_0_, f32[3,5120]{1,0:T(4,128)S(1)} %get-tuple-element.16.refs_1_, f32[3,5120]{1,0:T(4,128)S(1)} %get-tuple-element.17.refs_2_, ...), custom_call_target="tpu_custom_call" | custom-call | tf_op jit(solution)/shard_map/write_out/pallas_call | solution.py:400

commit v3 on v2

--- a/solution.py
+++ b/solution.py
@@ -26,7 +26,6 @@
 NEAR = (1, 3, 2)
 FAR = (2, 1, 3)
 Z_ORDER = (8, 7, 9, 6, 10, 5, 11, 4, 12, 3, 13, 2, 14, 1, 15)
-LAG = 4
 
 
 def constants():
@@ -134,7 +133,7 @@
             )
         )
     ]
-    steps = [(dx, e) for dx in FAR + (0,) for e in (1, 0)]
+    steps = [(dx, e) for e in (0, 1) for dx in FAR + (0,)]
 
     def cot_cols(dx, e):
         col = lax.rem(y_lo + e, 2) * 4 + lax.rem(x + dx, 4)
@@ -151,53 +150,47 @@
     for load in loads[2:]:
         load.start()
 
-    def local_term(t):
-        cot_load(t).wait()
-        grads[t] = dot(hidden_t, cot_v[:, cot_cols(*steps[t])])
-        pair_s[t] = grads[t, pl.ds(pl.multiple_of((1 - core) * 96, 16), 96), :].astype(BF16)
-
-    def pair_copy(t):
-        return send(pair_s.at[t], pair_r.at[t], 0, pair_sem.at[t], sibling)
-
-    def first_axis(t):
-        pair_copy(t).wait_recv()
-        dx, e = steps[t]
-        for dy in (e, e + 2):
-            row = lax.div(lax.rem(y + dy, 4), 2) * BR
-            a, b = jnp.where(first, dx, dy), jnp.where(first, dy, dx)
-
-            def term():
-                own = grads[t, pl.ds(pl.multiple_of(core * 96 + row, 16), BR), :]
-                return own + pair_r[t, pl.ds(pl.multiple_of(row, 16), BR), :].astype(F32)
-
-            def keep():
-                mine[b] = term()
-
-            def pass_on():
-                k = b * 3 + a - 1
-                one_s[k] = term().astype(BF16)
-                send(one_s.at[k], one_r.at[k], 1, one_sem.at[b], along_one(a)).start()
-
-            if dx and dy:
-                pass_on()
-            elif dx == dy:
-                keep()
-            else:
-                pl.when(a == 0)(keep)
-                pl.when(a != 0)(pass_on)
+    def pair_copy(k):
+        return send(pair_s.at[k], pair_r.at[k], 0, pair_sem.at[k], sibling)
 
     loads[0].wait()
     loads[1].wait()
     hidden_t = dot(order_v[...], hidden_v[...]).astype(BF16)
-    for t in range(8):
-        local_term(t)
+    for t, (dx, e) in enumerate(steps):
+        k = dx * 2 + e
+        cot_load(t).wait()
+        grads[k] = dot(hidden_t, cot_v[:, cot_cols(dx, e)])
+        pair_s[k] = grads[k, pl.ds(pl.multiple_of((1 - core) * 96, 16), 96), :].astype(BF16)
         if t == 0:
             pl.semaphore_wait(barrier, 1 + 6 + 4)
             signal(hello.at[0], along_z(2))
             signal(hello.at[0], along_z(NZ - 2))
-        pair_copy(t).start()
-        if t >= LAG:
-            first_axis(t - LAG)
+        pair_copy(k).start()
+
+    def first_axis(a, b):
+        dx, dy = jnp.where(first, a, b), jnp.where(first, b, a)
+        k = dx * 2 + lax.rem(dy, 2)
+        new_0, new_1 = b in (2, 1), a in (2, 1)
+        if new_0 and new_1:
+            pair_copy(k).wait_recv()
+        elif new_0 or new_1:
+            pl.when(first if new_0 else jnp.logical_not(first))(lambda: pair_copy(k).wait_recv())
+        row = pl.multiple_of(lax.div(lax.rem(y + dy, 4), 2) * BR, 16)
+        term = grads[k, pl.ds(pl.multiple_of(core * 96 + row, 16), BR), :] + pair_r[k, pl.ds(row, BR), :].astype(F32)
+        if a == 0:
+            mine[b] = term
+        else:
+            n = b * 3 + a - 1
+            one_s[n] = term.astype(BF16)
+            send(one_s.at[n], one_r.at[n], 1, one_sem.at[b], along_one(a)).start()
+
+    for b in FAR + (0,):
+        for a in FAR + (0,):
+            first_axis(a, b)
+        if b == 1:
+            pl.semaphore_wait(hello.at[0], 2)
+            signal(hello.at[1], along_z(4))
+            signal(hello.at[1], along_z(NZ - 4))
 
     for load in loads[2:]:
         load.wait()
@@ -208,11 +201,6 @@
             states[s, OWN * j : OWN * (j + 1), :] = ref[:, cols]
     w_z[z] = states[0].astype(BF16)
 
-    pl.semaphore_wait(hello.at[0], 2)
-    signal(hello.at[1], along_z(4))
-    signal(hello.at[1], along_z(NZ - 4))
-    for t in range(8 - LAG, 8):
-        first_axis(t)
     pl.semaphore_wait(hello.at[1], 2)
 
     def spread_z(ref, family, recv):
@@ -296,9 +284,6 @@
     rep_y = send(unit.at[pl.ds(0, 4)], unit.at[pl.ds(4, 4)], 13, rep_sem.at[1], other_y)
     rep_y.start()
 
-    for b in (0,) + NEAR:
-        gather_pair(w_own, w_sib, 4, w_sem, b)
-
     rep_y.wait_recv()
     for e in range(2):
         for d in range(4):
@@ -308,6 +293,9 @@
                 grad_rows[:, cols] = unit[e * 4 + d, OWN * j : OWN * (j + 1), :]
     new = adam_update(master_v[...], moment_v[...], second_v[...], grad_rows[...])
     master_out[...], moment_out[...], second_out[...] = new
+
+    for b in (0,) + NEAR:
+        gather_pair(w_own, w_sib, 4, w_sem, b)
 
     gather_z(u_z, u_own, u_sem)
     gather_two(u_own, 8, u_sem)

time: 66.1 us -> 57.9 us (0.88)
  Pallas kernels: 65.3 us -> 57.1 us
    pallas_call x1, Pallas kernels: 63.9 us -> 55.7 us  [local(): pl.pallas_call(functools.partial(kernel, factor), out_shape=(vmem((ROWS,...]
where the time goes in v3:
time: 57.9 us; the launch traced here: 57.7 us
  Pallas kernels  57.1 us (99%)
  between operations  0.64 us (1%)
    pallas_call x1, Pallas kernels, local(): pl.pallas_call(functools.partial(kernel, factor), out_shape=(vmem((ROWS,...  55.7 us
    pallas_call x1, Pallas kernels, local(): pl.pallas_call(write_out, out_shape=tuple((pltpu.HBM(r.shape, r.dtype) fo...  1.43 us

profile of v3, /device:TPU:1, one launch (start us, length us, event | category | flops | bytes accessed | tf_op | source)
XLA Modules:
  0.0 57.7 jit_solution(14241878158248623426)
XLA Ops:
  0.6 55.7 %adamw_step.1 = (bf16[192,256]{1,0:T(8,128)(2,1)S(1)}, f32[3,5120]{1,0:T(4,128)S(1)}, f32[3,5120]{1,0:T(4,128)S(1)}, f32[3,5120]{1,0:T(4,128)S(1)}, bf16[192,5120]{1,0:T(8,128)(2,1)S(1)}) custom-call(bf16[192,256]{1,0:T(8,128)(2,1)} %bitcast.2, bf16[256,5120]{1,0:T(8,128)(2,1)} %cot.1, f32[3,5120]{1,0:T(4,128)} %master.1, f32[3,5120]{1,0:T(4,128)} %moment.1, ...), custom_call_target="tpu_custom_call" | custom-call | tf_op jit(solution)/shard_map/adamw_step/pallas_call | solution.py:367
  56.3 1.4 %write_out.1 = (bf16[192,256]{1,0:T(8,128)(2,1)}, f32[3,5120]{1,0:T(4,128)}, f32[3,5120]{1,0:T(4,128)}, f32[3,5120]{1,0:T(4,128)}, bf16[192,5120]{1,0:T(8,128)(2,1)}) custom-call(bf16[192,256]{1,0:T(8,128)(2,1)S(1)} %get-tuple-element.15.refs_0_, f32[3,5120]{1,0:T(4,128)S(1)} %get-tuple-element.16.refs_1_, f32[3,5120]{1,0:T(4,128)S(1)} %get-tuple-element.17.refs_2_, ...), custom_call_target="tpu_custom_call" | custom-call | tf_op jit(solution)/shard_map/write_out/pallas_call | solution.py:388

commit v4 on v3

--- a/solution.py
+++ b/solution.py
@@ -25,6 +25,8 @@
 
 NEAR = (1, 3, 2)
 FAR = (2, 1, 3)
+Z_NEAR_FIRST = (0, 1, 15, 2, 14, 3, 13, 4, 12, 5, 11, 6, 10, 7, 9, 8)
+CUT = 32
 Z_ORDER = (8, 7, 9, 6, 10, 5, 11, 4, 12, 3, 13, 2, 14, 1, 15)
 
 
@@ -40,13 +42,23 @@
         for j in range(NJ):
             for i in range(OWN):
                 tiles[z * TILE + OWN * j + i, j * BR + z * OWN + i] = 1.0
-    weave = np.zeros((2, 96, 96), np.float32)
-    for core in range(2):
-        for c in range(2):
+    slots_a, slots_b = (0, 1, 2, 3, 4, 5, 11, 12, 13, 14, 15), (6, 7, 8, 9, 10, 11)
+    near = np.zeros((NJ * CUT, len(slots_a) * TILE), np.float32)
+    far = np.zeros((NJ * (BR - CUT), len(slots_b) * TILE), np.float32)
+    weave = np.zeros((NZ, 2, 96, 96), np.float32)
+    for n, d in enumerate(Z_NEAR_FIRST):
+        for i in range(OWN):
+            r = n * OWN + i
+            for j in range(NJ):
+                if r < CUT:
+                    near[j * CUT + r, slots_a.index(d) * TILE + OWN * j + i] = 1.0
+                else:
+                    far[j * (BR - CUT) + r - CUT, slots_b.index(d) * TILE + OWN * j + i] = 1.0
             for z in range(NZ):
-                for i in range(OWN):
-                    weave[core, z * 6 + c * OWN + i, (0 if c == core else BR) + z * OWN + i] = 1.0
-    return tuple(m.astype(BF16) for m in (order, tiles, tiles.T.copy(), weave))
+                for core in range(2):
+                    for c in range(2):
+                        weave[z, core, (z - d) % NZ * 6 + c * OWN + i, (0 if c == core else BR) + r] = 1.0
+    return tuple(m.astype(BF16) for m in (order, tiles, near, far, weave))
 
 
 def adam_update(master, moment, second, gradient):
@@ -72,11 +84,11 @@
 
 def kernel(
     factor,
-    hidden, cot, master, moment, second, order, tiles, tiles_t, weave,
+    hidden, cot, master, moment, second, order, tiles, tiles_a, tiles_b, weave,
     ig_out, master_out, moment_out, second_out, weights_out,
-    hidden_v, cot_v, master_v, moment_v, second_v, order_v, tiles_v, tiles_tv, weave_v,
+    hidden_v, cot_v, master_v, moment_v, second_v, order_v, tiles_v, tiles_av, tiles_bv, weave_v,
     states, grads, pair_s, pair_r, mine, one_s, one_r, two_s, two_r,
-    z_s, z_r, unit, w_z, u_z, w_own, w_sib, u_own, u_sib, w_full, grad_rows, ig_sum,
+    z_s, z_r, unit, w_z, u_z, w_own_a, w_sib_a, w_own_b, w_sib_b, u_own_a, u_sib_a, u_own_b, u_sib_b, w_full, grad_rows, ig_sum,
     in_sem, cot_sem, sent, pair_sem, one_sem, two_sem, z_sem, rep_sem, w_sem, u_sem, hello,
 ):
     rep, shard = lax.axis_index("rep"), lax.axis_index("shard")
@@ -109,14 +121,6 @@
 
     def signal(sem, to):
         pl.semaphore_signal(sem, inc=1, device_id=to, device_id_type=MESH)
-
-    barrier = pltpu.get_barrier_semaphore()
-    signal(barrier, sibling)
-    for d in (2, 1, 3):
-        signal(barrier, along_one(d))
-        signal(barrier, along_two(d))
-    for d in (2, NZ - 2, 1, NZ - 1):
-        signal(barrier, along_z(d))
 
     loads = [
         pltpu.make_async_copy(src, dst, in_sem.at[k])
@@ -128,12 +132,13 @@
                 (moment, moment_v),
                 (second, second_v),
                 (tiles, tiles_v),
-                (tiles_t, tiles_tv),
-                (weave, weave_v),
+                (tiles_a, tiles_av),
+                (tiles_b, tiles_bv),
+                (weave.at[z, core], weave_v),
             )
         )
     ]
-    steps = [(dx, e) for e in (0, 1) for dx in FAR + (0,)]
+    steps = [(dx, e) for dx in FAR + (0,) for e in (0, 1)]
 
     def cot_cols(dx, e):
         col = lax.rem(y_lo + e, 2) * 4 + lax.rem(x + dx, 4)
@@ -147,6 +152,13 @@
     loads[1].start()
     for t in range(8):
         cot_load(t).start()
+    barrier = pltpu.get_barrier_semaphore()
+    signal(barrier, sibling)
+    for d in (2, 1, 3):
+        signal(barrier, along_one(d))
+        signal(barrier, along_two(d))
+    for d in (2, NZ - 2, 1, NZ - 1):
+        signal(barrier, along_z(d))
     for load in loads[2:]:
         load.start()
 
@@ -156,7 +168,8 @@
     loads[0].wait()
     loads[1].wait()
     hidden_t = dot(order_v[...], hidden_v[...]).astype(BF16)
-    for t, (dx, e) in enumerate(steps):
+    def local_term(t):
+        dx, e = steps[t]
         k = dx * 2 + e
         cot_load(t).wait()
         grads[k] = dot(hidden_t, cot_v[:, cot_cols(dx, e)])
@@ -167,14 +180,19 @@
             signal(hello.at[0], along_z(NZ - 2))
         pair_copy(k).start()
 
+    seen = (set(), set())
+
     def first_axis(a, b):
         dx, dy = jnp.where(first, a, b), jnp.where(first, b, a)
         k = dx * 2 + lax.rem(dy, 2)
-        new_0, new_1 = b in (2, 1), a in (2, 1)
-        if new_0 and new_1:
+        new = []
+        for c, of_c in enumerate((a * 2 + b % 2, b * 2 + a % 2)):
+            new.append(of_c not in seen[c])
+            seen[c].add(of_c)
+        if new[0] and new[1]:
             pair_copy(k).wait_recv()
-        elif new_0 or new_1:
-            pl.when(first if new_0 else jnp.logical_not(first))(lambda: pair_copy(k).wait_recv())
+        elif new[0] or new[1]:
+            pl.when(first if new[0] else jnp.logical_not(first))(lambda: pair_copy(k).wait_recv())
         row = pl.multiple_of(lax.div(lax.rem(y + dy, 4), 2) * BR, 16)
         term = grads[k, pl.ds(pl.multiple_of(core * 96 + row, 16), BR), :] + pair_r[k, pl.ds(row, BR), :].astype(F32)
         if a == 0:
@@ -184,13 +202,21 @@
             one_s[n] = term.astype(BF16)
             send(one_s.at[n], one_r.at[n], 1, one_sem.at[b], along_one(a)).start()
 
+    for t in range(6):
+        local_term(t)
+    first_axis(2, 2)
+    first_axis(1, 2)
+    local_term(6)
+    first_axis(2, 1)
+    first_axis(1, 1)
+    local_term(7)
+    for a, b in ((3, 2), (3, 1), (2, 3), (1, 3), (3, 3), (2, 0), (1, 0), (3, 0)):
+        first_axis(a, b)
+    pl.semaphore_wait(hello.at[0], 2)
+    signal(hello.at[1], along_z(4))
+    signal(hello.at[1], along_z(NZ - 4))
     for b in FAR + (0,):
-        for a in FAR + (0,):
-            first_axis(a, b)
-        if b == 1:
-            pl.semaphore_wait(hello.at[0], 2)
-            signal(hello.at[1], along_z(4))
-            signal(hello.at[1], along_z(NZ - 4))
+        first_axis(0, b)
 
     for load in loads[2:]:
         load.wait()
@@ -199,15 +225,16 @@
         for j in range(NJ):
             cols = pl.ds(pl.multiple_of(rep * BC + j * 128, 128), 128)
             states[s, OWN * j : OWN * (j + 1), :] = ref[:, cols]
-    w_z[z] = states[0].astype(BF16)
+    w_z[0] = states[0].astype(BF16)
 
     pl.semaphore_wait(hello.at[1], 2)
 
-    def spread_z(ref, family, recv):
+    def spread_z(ref, family, sem):
         for d in Z_ORDER:
-            send(ref.at[z], ref.at[z], family, recv, along_z(d)).start()
-
-    spread_z(w_z, 4, w_sem.at[0])
+            where = sem.at[1] if 6 <= d <= 10 else sem.at[0]
+            send(ref.at[0], ref.at[d], family, where, along_z(d)).start()
+
+    spread_z(w_z, 4, w_sem)
 
     for b in FAR + (0,):
         received(one_r.at[3 * b : 3 * b + 3], one_sem.at[b])
@@ -230,43 +257,61 @@
     for d in Z_ORDER:
         send(z_s.at[lax.rem(z + d, NZ)], z_r.at[d - 1], 3, z_sem.at[0], along_z(d)).start()
 
-    def gather_z(ref, own, sem):
-        received(ref.at[0 : NZ - 1], sem.at[0])
-        pieces = dot(tiles_tv[...], ref[...].reshape(NZ * TILE, 128)).astype(BF16)
+    def gather_near(ref, own, sem):
+        received(ref.at[1:11], sem.at[0])
+        parts = jnp.concatenate([ref[0:6].reshape(6 * TILE, 128), ref[11:16].reshape(5 * TILE, 128)], axis=0)
+        pieces = dot(tiles_av[...], parts).astype(BF16)
         for j in range(NJ):
-            own[0, :, j * 128 : (j + 1) * 128] = pieces[j * BR : (j + 1) * BR]
-
-    def gather_two(own, family, sem):
+            own[0, :, j * 128 : (j + 1) * 128] = pieces[j * CUT : (j + 1) * CUT]
+
+    def gather_far(ref, own, sem):
+        received(ref.at[6:11], sem.at[1])
+        pieces = dot(tiles_bv[...], ref[6:12].reshape(6 * TILE, 128)).astype(BF16)
+        rows = BR - CUT
+        for j in range(NJ):
+            own[0, :, j * 128 : (j + 1) * 128] = pieces[j * rows : (j + 1) * rows]
+
+    def gather_two(part):
+        own, _, family, sem, s = part
         for b in FAR:
-            send(own.at[0], own.at[4 * b], family + 1, sem.at[b], along_two(b)).start()
-
-    def gather_one(own, family, sem, b):
+            send(own.at[0], own.at[4 * b], family, sem.at[s + b], along_two(b)).start()
+
+    def gather_one(part, b):
+        own, _, family, sem, s = part
         if b:
-            received(own.at[4 * b], sem.at[b])
+            received(own.at[4 * b], sem.at[s + b])
         for a in FAR:
-            send(own.at[4 * b], own.at[4 * b + a], family + 2, sem.at[4 + b], along_one(a)).start()
-
-    def gather_pair(own, sib, family, sem, b):
-        received(own.at[4 * b + 1 : 4 * b + 4], sem.at[4 + b])
+            send(own.at[4 * b], own.at[4 * b + a], family + 1, sem.at[s + 4 + b], along_one(a)).start()
+
+    def gather_pair(part, b):
+        own, sib, family, sem, s = part
+        received(own.at[4 * b + 1 : 4 * b + 4], sem.at[s + 4 + b])
         four = pl.ds(4 * b, 4)
-        send(own.at[four], sib.at[four], family + 3, sem.at[8 + b], sibling).start()
-
-    def pair_there(sib, sem, b):
-        received(sib.at[4 * b : 4 * b + 4], sem.at[8 + b])
-
-    def place(own, sib, full, dx, dy):
+        send(own.at[four], sib.at[four], family + 2, sem.at[s + 8 + b], sibling).start()
+
+    def pair_there(part, b):
+        _, sib, _, sem, s = part
+        received(sib.at[4 * b : 4 * b + 4], sem.at[s + 8 + b])
+
+    w_parts = ((w_own_a, w_sib_a, 5, w_sem, 2), (w_own_b, w_sib_b, 8, w_sem, 14))
+    u_parts = ((u_own_a, u_sib_a, 12, u_sem, 2), (u_own_b, u_sib_b, 15, u_sem, 14))
+
+    def place(parts, full, dx, dy):
         from_x, from_y = lax.rem(x + 4 - dx, 4), lax.rem(y + 4 - dy, 4)
         k_own = jnp.where(first, dy * 4 + dx, dx * 4 + dy)
         k_sib = jnp.where(first, dx * 4 + dy, dy * 4 + dx)
-        both = jnp.concatenate([own[k_own], sib[k_sib]], axis=0)
+        both = jnp.concatenate([p[0][k_own] for p in parts] + [p[1][k_sib] for p in parts], axis=0)
         rows = pl.ds(pl.multiple_of(lax.div(from_y, 2) * 96, 16), 96)
         cols = pl.ds(pl.multiple_of((lax.rem(from_y, 2) * 4 + from_x) * BC, 128), BC)
-        full[rows, cols] = dot(weave_v[core], both).astype(BF16)
-
-    gather_z(w_z, w_own, w_sem)
-    gather_two(w_own, 4, w_sem)
+        full[rows, cols] = dot(weave_v[...], both).astype(BF16)
+
+    gather_near(w_z, w_own_a, w_sem)
+    gather_two(w_parts[0])
+    gather_far(w_z, w_own_b, w_sem)
+    gather_two(w_parts[1])
     for b in (0,) + NEAR:
-        gather_one(w_own, 4, w_sem, b)
+        for part in w_parts:
+            gather_one(part, b)
 
     received(z_r, z_sem.at[0])
     term = z_s[z].astype(F32)
@@ -274,15 +319,25 @@
         term += z_r[k].astype(F32)
     gradient = term * factor
     unit[0] = gradient
-    u_z[z] = adam_update(states[0], states[1], states[2], gradient)[0].astype(BF16)
-    spread_z(u_z, 8, u_sem.at[0])
+    u_z[0] = adam_update(states[0], states[1], states[2], gradient)[0].astype(BF16)
+    spread_z(u_z, 11, u_sem)
 
     for d in FAR:
-        send(unit.at[0], unit.at[d], 12, rep_sem.at[0], at_xy(d, 0)).start()
+        send(unit.at[0], unit.at[d], 18, rep_sem.at[0], at_xy(d, 0)).start()
     received(unit.at[1:4], rep_sem.at[0])
     other_y = device(x, y + 1 - 2 * y_lo, z, core)
-    rep_y = send(unit.at[pl.ds(0, 4)], unit.at[pl.ds(4, 4)], 13, rep_sem.at[1], other_y)
+    rep_y = send(unit.at[pl.ds(0, 4)], unit.at[pl.ds(4, 4)], 19, rep_sem.at[1], other_y)
     rep_y.start()
+
+    gather_near(u_z, u_own_a, u_sem)
+    gather_two(u_parts[0])
+    gather_one(u_parts[0], 0)
+    gather_far(u_z, u_own_b, u_sem)
+    gather_two(u_parts[1])
+    gather_one(u_parts[1], 0)
+    for b in (0,) + NEAR:
+        for part in w_parts:
+            gather_pair(part, b)
 
     rep_y.wait_recv()
     for e in range(2):
@@ -294,19 +349,15 @@
     new = adam_update(master_v[...], moment_v[...], second_v[...], grad_rows[...])
     master_out[...], moment_out[...], second_out[...] = new
 
-    for b in (0,) + NEAR:
-        gather_pair(w_own, w_sib, 4, w_sem, b)
-
-    gather_z(u_z, u_own, u_sem)
-    gather_two(u_own, 8, u_sem)
-    gather_one(u_own, 8, u_sem, 0)
+    for b in NEAR:
+        for part in u_parts:
+            gather_one(part, b)
     for b in range(4):
-        pair_there(w_sib, w_sem, b)
+        for part in w_parts:
+            pair_there(part, b)
     for dx in range(4):
         for dy in range(4):
-            place(w_own, w_sib, w_full, dx, dy)
-    for b in NEAR:
-        gather_one(u_own, 8, u_sem, b)
+            place(w_parts, w_full, dx, dy)
 
     ig_sum[...] = dot_t(w_full[:, 0:BC], cot_v[:, 0:BC])
 
@@ -327,19 +378,20 @@
     bs = (0,) + NEAR
     for k in range(5):
         if k < 4:
-            gather_pair(u_own, u_sib, 8, u_sem, bs[k])
+            for part in u_parts:
+                gather_pair(part, bs[k])
         if k > 0:
-            pair_there(u_sib, u_sem, bs[k - 1])
+            for part in u_parts:
+                pair_there(part, bs[k - 1])
             for dx, dy in ready[k - 1]:
-                place(u_own, u_sib, weights_out, dx, dy)
-
-    tiles_of = lambda ref: ref.at[0 : NZ - 1]
-    for family, ref in (
-        (0, pair_s), (1, one_s), (2, two_s), (3, z_r),
-        (4, tiles_of(w_z)), (5, w_own.at[0:3]), (6, w_own.at[0:12]), (7, w_own),
-        (8, tiles_of(u_z)), (9, u_own.at[0:3]), (10, u_own.at[0:12]), (11, u_own),
-        (12, unit.at[1:4]), (13, unit.at[0:4]),
-    ):
+                place(u_parts, weights_out, dx, dy)
+
+    leaving = [(0, pair_s), (1, one_s), (2, two_s), (3, z_r), (18, unit.at[1:4]), (19, unit.at[0:4])]
+    for parts, ref, family in ((w_parts, w_z, 4), (u_parts, u_z, 11)):
+        leaving.append((family, ref.at[0 : NZ - 1]))
+        for own, _, first_family, _, _ in parts:
+            leaving += [(first_family, own.at[0:3]), (first_family + 1, own.at[0:12]), (first_family + 2, own)]
+    for family, ref in leaving:
         send(ref, ref, family, pair_sem.at[0], sibling).wait_send()
 
 
@@ -359,6 +411,7 @@
     vmem = pltpu.VMEM
     dma = pltpu.SemaphoreType.DMA
     blocks = lambda n, dtype=BF16: vmem((n, BR, BC), dtype)
+    near, far = vmem((16, CUT, BC), BF16), vmem((16, BR - CUT, BC), BF16)
     z_tiles = lambda n, dtype=BF16: vmem((n, TILE, 128), dtype)
     owned = vmem((OWN, D), F32)
     pairs = vmem((8, 2 * BR, BC), BF16)
@@ -367,18 +420,18 @@
     results = pl.pallas_call(
         functools.partial(kernel, factor),
         out_shape=(vmem((ROWS, TOK), BF16), owned, owned, owned, vmem((ROWS, D), BF16)),
-        in_specs=[pl.BlockSpec(memory_space=pltpu.HBM)] * 9,
+        in_specs=[pl.BlockSpec(memory_space=pltpu.HBM)] * (5 + len(consts)),
         out_specs=(pl.BlockSpec(memory_space=vmem),) * 5,
         scratch_shapes=[
             vmem((ROWS, TOK), BF16), vmem((TOK, D), BF16), owned, owned, owned,
-            *(vmem(m.shape, BF16) for m in consts),
+            *(vmem(m.shape[-2:], BF16) for m in consts),
             z_tiles(3, F32), vmem((8, ROWS, BC), F32), pairs, pairs, blocks(4, F32),
             blocks(12), blocks(12), blocks(3), blocks(3),
             z_tiles(NZ), z_tiles(NZ - 1), z_tiles(8, F32), z_tiles(NZ), z_tiles(NZ),
-            blocks(16), blocks(16), blocks(16), blocks(16),
+            *((near, near, far, far) * 2),
             vmem((ROWS, D), BF16), owned, vmem((ROWS, TOK), F32),
-            dma((8,)), dma((8,)), dma((14,)), dma((8,)), dma((4,)), dma((1,)), dma((1,)), dma((2,)),
-            dma((12,)), dma((12,)), pltpu.SemaphoreType.REGULAR((2,)),
+            dma((9,)), dma((8,)), dma((20,)), dma((8,)), dma((4,)), dma((1,)), dma((1,)), dma((2,)),
+            dma((26,)), dma((26,)), pltpu.SemaphoreType.REGULAR((2,)),
         ],
         compiler_params=pltpu.CompilerParams(
             collective_id=0, has_side_effects=True, vmem_limit_bytes=40 * 2**20

time: 57.9 us -> 55.4 us (0.957)
  Pallas kernels: 57.1 us -> 54.6 us
    pallas_call x1, Pallas kernels: 55.7 us -> 53.1 us  [local(): pl.pallas_call(functools.partial(kernel, factor), out_shape=(vmem((ROWS,...]
where the time goes in v4:
time: 55.4 us; the launch traced here: 55.2 us
  Pallas kernels  54.6 us (99%)
  between operations  0.64 us (1%)
    pallas_call x1, Pallas kernels, local(): pl.pallas_call(functools.partial(kernel, factor), out_shape=(vmem((ROWS,...  53.1 us
    pallas_call x1, Pallas kernels, local(): pl.pallas_call(write_out, out_shape=tuple((pltpu.HBM(r.shape, r.dtype) fo...  1.43 us

profile of v4, /device:TPU:1, one launch (start us, length us, event | category | flops | bytes accessed | tf_op | source)
XLA Modules:
  0.0 55.2 jit_solution(7080227332636415077)
XLA Ops:
  0.6 53.1 %adamw_step.1 = (bf16[192,256]{1,0:T(8,128)(2,1)S(1)}, f32[3,5120]{1,0:T(4,128)S(1)}, f32[3,5120]{1,0:T(4,128)S(1)}, f32[3,5120]{1,0:T(4,128)S(1)}, bf16[192,5120]{1,0:T(8,128)(2,1)S(1)}) custom-call(bf16[192,256]{1,0:T(8,128)(2,1)} %bitcast.2, bf16[256,5120]{1,0:T(8,128)(2,1)} %cot.1, f32[3,5120]{1,0:T(4,128)} %master.1, f32[3,5120]{1,0:T(4,128)} %moment.1, ...), custom_call_target="tpu_custom_call" | custom-call | tf_op jit(solution)/shard_map/adamw_step/pallas_call | solution.py:420
  53.8 1.4 %write_out.1 = (bf16[192,256]{1,0:T(8,128)(2,1)}, f32[3,5120]{1,0:T(4,128)}, f32[3,5120]{1,0:T(4,128)}, f32[3,5120]{1,0:T(4,128)}, bf16[192,5120]{1,0:T(8,128)(2,1)}) custom-call(bf16[192,256]{1,0:T(8,128)(2,1)S(1)} %get-tuple-element.15.refs_0_, f32[3,5120]{1,0:T(4,128)S(1)} %get-tuple-element.16.refs_1_, f32[3,5120]{1,0:T(4,128)S(1)} %get-tuple-element.17.refs_2_, ...), custom_call_target="tpu_custom_call" | custom-call | tf_op jit(solution)/shard_map/write_out/pallas_call | solution.py:441

commit v5 on v4

--- a/solution.py
+++ b/solution.py
@@ -349,8 +349,8 @@
     new = adam_update(master_v[...], moment_v[...], second_v[...], grad_rows[...])
     master_out[...], moment_out[...], second_out[...] = new
 
-    for b in NEAR:
-        for part in u_parts:
+    for part in u_parts:
+        for b in NEAR:
             gather_one(part, b)
     for b in range(4):
         for part in w_parts:
@@ -376,10 +376,11 @@
         ((0, 2), (2, 0), (1, 2), (2, 1), (3, 2), (2, 3), (2, 2)),
     )
     bs = (0,) + NEAR
+    for b in bs:
+        gather_pair(u_parts[0], b)
     for k in range(5):
         if k < 4:
-            for part in u_parts:
-                gather_pair(part, bs[k])
+            gather_pair(u_parts[1], bs[k])
         if k > 0:
             for part in u_parts:
                 pair_there(part, bs[k - 1])

time: 55.4 us -> 54.9 us (level)
  no operation moved by 1% of the time
where the time goes in v5:
time: 54.9 us; the launch traced here: 54.7 us
  Pallas kernels  54.1 us (99%)
  between operations  0.64 us (1%)
    pallas_call x1, Pallas kernels, local(): pl.pallas_call(functools.partial(kernel, factor), out_shape=(vmem((ROWS,...  52.7 us
    pallas_call x1, Pallas kernels, local(): pl.pallas_call(write_out, out_shape=tuple((pltpu.HBM(r.shape, r.dtype) fo...  1.43 us

profile of v5, /device:TPU:1, one launch (start us, length us, event | category | flops | bytes accessed | tf_op | source)
XLA Modules:
  0.0 54.7 jit_solution(8075894907776735726)
XLA Ops:
  0.6 52.7 %adamw_step.1 = (bf16[192,256]{1,0:T(8,128)(2,1)S(1)}, f32[3,5120]{1,0:T(4,128)S(1)}, f32[3,5120]{1,0:T(4,128)S(1)}, f32[3,5120]{1,0:T(4,128)S(1)}, bf16[192,5120]{1,0:T(8,128)(2,1)S(1)}) custom-call(bf16[192,256]{1,0:T(8,128)(2,1)} %bitcast.2, bf16[256,5120]{1,0:T(8,128)(2,1)} %cot.1, f32[3,5120]{1,0:T(4,128)} %master.1, f32[3,5120]{1,0:T(4,128)} %moment.1, ...), custom_call_target="tpu_custom_call" | custom-call | tf_op jit(solution)/shard_map/adamw_step/pallas_call | solution.py:421
  53.3 1.4 %write_out.1 = (bf16[192,256]{1,0:T(8,128)(2,1)}, f32[3,5120]{1,0:T(4,128)}, f32[3,5120]{1,0:T(4,128)}, f32[3,5120]{1,0:T(4,128)}, bf16[192,5120]{1,0:T(8,128)(2,1)}) custom-call(bf16[192,256]{1,0:T(8,128)(2,1)S(1)} %get-tuple-element.15.refs_0_, f32[3,5120]{1,0:T(4,128)S(1)} %get-tuple-element.16.refs_1_, f32[3,5120]{1,0:T(4,128)S(1)} %get-tuple-element.17.refs_2_, ...), custom_call_target="tpu_custom_call" | custom-call | tf_op jit(solution)/shard_map/write_out/pallas_call | solution.py:442
